TPU v7x, 512 devices: a whole 4x4x16 slice. The times are simulated.
512 devices in a mesh: prompt: 16 (over y, x_lo, core), group: 16 (over z), mp: 2 (over x_hi).
Axes of the slice: x: 4 (x_hi: 2, x_lo: 2; x = x_hi * 2 + x_lo), y: 4, z: 16, core: 2. Of those that a mesh axis runs over, the one named last changes fastest.
Arguments:
- action_queries: bfloat16 [16, 48, 50, 3584], P('prompt', 'group', None, 'mp'), may hold values from -6 to 6
- action_keys: bfloat16 [16, 48, 50, 3584], P('prompt', 'group', None, 'mp'), may hold values from -6 to 6
- action_values: bfloat16 [16, 48, 50, 3584], P('prompt', 'group', None, 'mp'), may hold values from -6 to 6
- upstream_grad: bfloat16 [16, 48, 50, 3584], P('prompt', 'group', None, 'mp'), may hold values from -6 to 6
- prefix_keys: bfloat16 [16, 128, 3584], P('prompt', 'group', 'mp'), may hold values from -6 to 6
- prefix_values: bfloat16 [16, 128, 3584], P('prompt', 'group', 'mp'), may hold values from -6 to 6
- prefix_mask: int32 [16, 128], P('prompt', 'group'), may hold values 0 or 1
- lengths: int32 [16, 48], P('prompt', 'group'), may hold values from 1 to 50, as said below
- rewards: int32 [16, 48], P('prompt', 'group'), may hold values from 0 to 24
- norm_gain: bfloat16 [3584], P('mp'), may hold values from 0.099609375 to 1.8984375
Outputs:
- grad_queries: bfloat16 [16, 48, 50, 3584], P('prompt', 'group', None, 'mp')
- grad_action_keys: bfloat16 [16, 48, 50, 3584], P('prompt', 'group', None, 'mp')
- grad_action_values: bfloat16 [16, 48, 50, 3584], P('prompt', 'group', None, 'mp')
- grad_prefix_keys: bfloat16 [16, 128, 3584], P('prompt', 'group', 'mp')
- grad_prefix_values: bfloat16 [16, 128, 3584], P('prompt', 'group', 'mp')
Inputs may be any that keep to these rules, and one draw needn't show every extreme that they name: `lengths`: the last sample of every prompt has exactly 50 live tokens.
All inputs are finite; a program needn't handle non-finite values. No bound on the sum of `prefix_mask` on one device may be relied on, other than what follows from the above.
Results may differ from a plain program's by a relative error of at most 0.025.
Values may be sent and summed in bfloat16 or wider, within the bound.
A program may use at most 64 MiB of HBM per device.

v0:
```python
import jax
import jax.numpy as jnp
from jax import lax
from jax.sharding import PartitionSpec as P

HEAD_DIM = 128


masked_score = -1e30
epsilon = 1e-06


def body(
    action_queries,
    action_keys,
    action_values,
    upstream_grad,
    prefix_keys,
    prefix_values,
    prefix_mask,
    lengths,
    rewards,
    norm_gain,
):
    floats = jnp.float32
    samp_here = action_queries.shape[1]
    act_len = action_queries.shape[2]
    width = action_queries.shape[3]
    heads = width // HEAD_DIM
    pre_here = prefix_keys.shape[1]
    scale = HEAD_DIM ** (-0.5)
    width_all = width * lax.axis_size("mp")
    live = jnp.arange(act_len)[None, :] < lengths[0][:, None]
    live_here = jnp.sum(live.astype(floats))
    reward_vals = rewards[0].astype(floats)
    reward_sum_here = jnp.sum(reward_vals)
    reward_sq_here = jnp.sum(reward_vals * reward_vals)
    reward_sum, reward_sq = lax.psum((reward_sum_here, reward_sq_here), "group")
    total_live = lax.psum(live_here, ("prompt", "group"))
    group_samples = samp_here * lax.axis_size("group")
    slots_all = lax.axis_size("prompt") * group_samples * act_len
    loss_scale = slots_all / total_live
    sum_int = reward_sum.astype(jnp.int32)
    sq_int = reward_sq.astype(jnp.int32)
    spread = jnp.sqrt((group_samples * sq_int - sum_int * sum_int).astype(floats)) / group_samples
    centre = sum_int.astype(floats) / group_samples
    advantage = (reward_vals - centre) / (spread + 1.0)
    weights = jnp.where(live, (advantage * loss_scale)[:, None], jnp.float32(0.0))
    q_heads = action_queries[0].reshape(samp_here, act_len, heads, HEAD_DIM)
    ka_heads = action_keys[0].reshape(samp_here, act_len, heads, HEAD_DIM)
    va_heads = action_values[0].reshape(samp_here, act_len, heads, HEAD_DIM)
    mask_wire = prefix_mask.astype(jnp.bfloat16)
    gathered = (
        lax.all_gather(prefix_keys, "group", axis=1, tiled=True),
        lax.all_gather(prefix_values, "group", axis=1, tiled=True),
        lax.all_gather(mask_wire, "group", axis=1, tiled=True),
    )
    prefix_len = gathered[0].shape[1]
    kp_heads = gathered[0][0].reshape(prefix_len, heads, HEAD_DIM)
    vp_heads = gathered[1][0].reshape(prefix_len, heads, HEAD_DIM)
    pre_live = gathered[2][0] > 0
    scores_pre = (
        jnp.einsum("stha,jha->hstj", q_heads, kp_heads, preferred_element_type=floats) * scale
    )
    scores_pre = jnp.where(pre_live[None, None, None, :], scores_pre, masked_score)
    causal = jnp.arange(act_len)[:, None] >= jnp.arange(act_len)[None, :]
    scores_act = (
        jnp.einsum("stha,suha->hstu", q_heads, ka_heads, preferred_element_type=floats) * scale
    )
    scores_act = jnp.where(causal, scores_act, masked_score)
    highest = jnp.maximum(jnp.max(scores_pre, -1), jnp.max(scores_act, -1))
    exp_pre = jnp.exp(scores_pre - highest[..., None])
    exp_act = jnp.exp(scores_act - highest[..., None])
    totals = jnp.sum(exp_pre, -1) + jnp.sum(exp_act, -1)
    probs_pre = (exp_pre / totals[..., None]).astype(jnp.bfloat16)
    probs_act = (exp_act / totals[..., None]).astype(jnp.bfloat16)
    attended = jnp.einsum(
        "hstj,jha->stha", probs_pre, vp_heads, preferred_element_type=floats
    ) + jnp.einsum("hstu,suha->stha", probs_act, va_heads, preferred_element_type=floats)
    gain_heads = norm_gain.astype(floats).reshape(heads, HEAD_DIM)
    upstream = upstream_grad[0].reshape(samp_here, act_len, heads, HEAD_DIM)
    scaled_up = gain_heads * upstream.astype(floats) * weights[:, :, None, None]
    squares_here = jnp.sum(attended * attended, axis=(2, 3))
    inner_here = jnp.sum(attended * scaled_up, axis=(2, 3))
    squares, inner = lax.psum((squares_here, inner_here), "mp")
    inverse = lax.rsqrt(squares / width_all + epsilon)
    factor = inverse * inverse * inner / width_all
    grad_att = (inverse[..., None, None] * (scaled_up - attended * factor[..., None, None])).astype(
        jnp.bfloat16
    )
    delta = jnp.sum(grad_att.astype(floats) * attended, -1).transpose(2, 0, 1)
    dprob_pre = jnp.einsum("stha,jha->hstj", grad_att, vp_heads, preferred_element_type=floats)
    dprob_act = jnp.einsum("stha,suha->hstu", grad_att, va_heads, preferred_element_type=floats)
    dscore_pre = (probs_pre.astype(floats) * (dprob_pre - delta[..., None])).astype(jnp.bfloat16)
    dscore_act = (probs_act.astype(floats) * (dprob_act - delta[..., None])).astype(jnp.bfloat16)
    grad_query = (
        jnp.einsum("hstj,jha->stha", dscore_pre, kp_heads, preferred_element_type=floats)
        + jnp.einsum("hstu,suha->stha", dscore_act, ka_heads, preferred_element_type=floats)
    ) * scale
    grad_keys = (
        jnp.einsum("hstu,stha->suha", dscore_act, q_heads, preferred_element_type=floats) * scale
    )
    grad_values = jnp.einsum("hstu,stha->suha", probs_act, grad_att, preferred_element_type=floats)
    value_part = jnp.einsum("hstj,stha->jha", probs_pre, grad_att, preferred_element_type=floats)
    key_part = (
        jnp.einsum("hstj,stha->jha", dscore_pre, q_heads, preferred_element_type=floats) * scale
    )
    summed = lax.psum_scatter(
        jnp.concatenate(
            [
                key_part.reshape(pre_here * lax.axis_size("group"), width),
                value_part.reshape(pre_here * lax.axis_size("group"), width),
            ],
            axis=1,
        ).astype(jnp.bfloat16),
        "group",
        scatter_dimension=0,
        tiled=True,
    ).astype(jnp.float32)
    grad_pre_keys = summed[:, :width].astype(jnp.bfloat16)[None]
    grad_pre_values = summed[:, width:].astype(jnp.bfloat16)[None]
    return (
        grad_query.reshape(1, samp_here, act_len, width).astype(jnp.bfloat16),
        grad_keys.reshape(1, samp_here, act_len, width).astype(jnp.bfloat16),
        grad_values.reshape(1, samp_here, act_len, width).astype(jnp.bfloat16),
        grad_pre_keys,
        grad_pre_values,
    )


def solution(mesh):
    return jax.shard_map(
        body,
        mesh=mesh,
        in_specs=(
            P("prompt", "group", None, "mp"),
            P("prompt", "group", None, "mp"),
            P("prompt", "group", None, "mp"),
            P("prompt", "group", None, "mp"),
            P("prompt", "group", "mp"),
            P("prompt", "group", "mp"),
            P("prompt", "group"),
            P("prompt", "group"),
            P("prompt", "group"),
            P("mp"),
        ),
        out_specs=(
            P("prompt", "group", None, "mp"),
            P("prompt", "group", None, "mp"),
            P("prompt", "group", None, "mp"),
            P("prompt", "group", "mp"),
            P("prompt", "group", "mp"),
        ),
        check_vma=False,
    )
```

profile of v0, /device:TPU:24, one launch (start us, length us, event | category | flops | bytes accessed | tf_op | source)
XLA Modules:
  0.0 780.0 jit_solution(16026811489856989105)
XLA Ops:
  7.3 1.6 reshape_squeeze.16
  8.9 38.2 %all_gather.10 = bf16[1,128,1792]{2,1,0:T(8,128)(2,1)S(1)} all-gather(bf16[1,8,1792]{2,1,0:T(8,128)(2,1)S(1)} %copy-done.13), channel_id=1, replica_groups=mesh['prompt'=16,'group'=16,'mp'=2] {'group'}, dimensions={1}, use_global_device_ids=true | all-gather | bytes 487424 | tf_op jit(solution)/shard_map/all_gather | solution.py:54
  47.0 0.3 copy.61
  47.4 1.3 dynamic-slice
  49.3 0.2 dynamic-update-slice
  49.6 27.0 %all-reduce = bf16[128]{0:T(256)(128)(2,1)S(1)} all-reduce(bf16[128]{0:T(256)(128)(2,1)S(1)} %dynamic-update-slice), channel_id=1, replica_groups=mesh['prompt'=16,'group'=16,'mp'=2] {'group'}, use_global_device_ids=true, to_apply=%add | all-reduce | flops 128 | bytes 512
  76.6 0.4 reshape_squeeze.18
  77.1 0.6 fusion.31
  77.7 0.6 fusion.32
  78.3 0.3 fusion.18
  78.6 0.8 fusion.17
  79.3 0.8 divide_convert_fusion.1
  80.2 0.3 divide_convert_fusion
  80.5 0.4 copy-done.16
  80.8 0.6 convert_reduce_fusion.1
  81.4 29.7 %all-reduce.1 = (f32[]{:T(128)}, f32[]{:T(128)}) all-reduce(f32[]{:T(128)} %get-tuple-element.8, f32[]{:T(128)} %get-tuple-element.7), channel_id=1, replica_groups=mesh['prompt'=16,'group'=16,'mp'=2] {'group'}, use_global_device_ids=true, to_apply=%region_9.10 | all-reduce | flops 2 | bytes 16 | tf_op jit(solution)/shard_map/psum | solution.py:38
  111.8 28.4 %all_gather.11 = bf16[1,128,1792]{2,1,0:T(8,128)(2,1)S(1)} all-gather(bf16[1,8,1792]{2,1,0:T(8,128)(2,1)S(1)} %copy-done.14), channel_id=1, replica_groups=mesh['prompt'=16,'group'=16,'mp'=2] {'group'}, dimensions={1}, use_global_device_ids=true | all-gather | bytes 487424 | tf_op jit(solution)/shard_map/all_gather | solution.py:55
  140.1 0.3 copy.66
  141.2 0.7 convert_reduce_fusion
  141.9 475.0 %psum.38 = f32[]{:T(128)} all-reduce(f32[]{:T(128)} %convert_reduce_fusion), channel_id=1, replica_groups=mesh['prompt'=16,'group'=16,'mp'=2] {'prompt','group'}, use_global_device_ids=true, to_apply=%region_11.12 | all-reduce | flops 1 | bytes 8 | tf_op jit(solution)/shard_map/psum | solution.py:39
  617.7 1.5 reshape.141
  619.1 1.3 reshape_squeeze.20
  620.4 0.5 convolution_bitcast_fusion.3
  620.9 0.6 copy-done
  621.5 2.0 multiply_reduce_fusion.2
  623.5 6.6 all-reduce.2
  630.1 2.0 multiply_reduce_fusion
  632.1 0.5 fusion.12
  632.6 0.2 copy.86
  632.8 0.5 fusion.10
  633.3 0.6 copy-done.9
  633.8 0.5 fusion.13
  634.3 0.2 copy.85
  634.5 0.1 copy-done.4
  634.7 1.0 pad_maximum_fusion
  635.7 0.5 fusion.14
  636.1 0.1 copy.83
  636.3 1.2 convert_element_type.133
  637.5 0.5 fusion.7
  638.0 0.6 copy-done.10
  638.6 0.5 fusion.15
  639.2 1.2 convert_element_type.130
  640.4 0.5 convolution_bitcast_fusion.2
  640.9 0.6 copy-done.3
  641.5 0.6 fusion.9
  642.2 1.2 convert_element_type.127
  643.4 128.4 %reduce-scatter.2.cloned.1.call-done = bf16[8,3584]{1,0:T(8,128)(2,1)} async-done(((bf16[128,3584]{1,0:T(8,128)(2,1)}), bf16[8,3584]{1,0:T(8,128)(2,1)}) %reduce-scatter.2.cloned.1.call-update) | async-done | bytes 57360 | tf_op jit(solution)/shard_map/reduce_scatter | solution.py:108
  771.8 1.4 slice_bitcast_fusion
  (46 shorter events, 0.5 us)
Async XLA Ops:
  7.2 1.7 copy-start.13
  7.2 764.6 %reduce-scatter.2.cloned.1.call-start = ((), (), s32[]{:S(2)}) async-start(), calls=%async_computation.1 | async-start | bytes 974848 | tf_op jit(solution)/shard_map/reduce_scatter | solution.py:108
  7.2 40.1 %copy-start.18 = (s32[1,8]{1,0:T(1,128)S(1)}, s32[1,8]{1,0:T(1,128)}, u32[]{:S(2)}) copy-start(s32[1,8]{1,0:T(1,128)} %param.16) | copy-start | bytes 100
  7.3 69.4 %copy-start.11 = (bf16[1,3,50,1792]{3,2,1,0:T(8,128)(2,1)S(1)}, bf16[1,3,50,1792]{3,2,1,0:T(8,128)(2,1)}, u32[]{:S(2)}) copy-start(bf16[1,3,50,1792]{3,2,1,0:T(8,128)(2,1)} %param.11) | copy-start | bytes 1612804
  8.8 68.8 %copy-start.8 = (bf16[3,50,14,128]{3,2,1,0:T(8,128)(2,1)}, bf16[3,50,14,128]{3,2,1,0:T(8,128)(2,1)S(1)}, u32[]{:S(2)}) copy-start(bf16[3,50,14,128]{3,2,1,0:T(8,128)(2,1)S(1)} %reshape_squeeze.16) | copy-start | bytes 1612804
  47.3 30.3 %copy-start.6 = (bf16[1,128,1792]{1,2,0:T(8,128)(2,1)}, bf16[1,128,1792]{1,2,0:T(8,128)(2,1)S(1)}, u32[]{:S(2)}) copy-start(bf16[1,128,1792]{1,2,0:T(8,128)(2,1)S(1)} %copy.61) | copy-start | bytes 1376260
  77.1 1.2 copy-start.2
  80.2 0.7 copy-start.16
  80.2 31.6 %copy-start.14 = (bf16[1,8,1792]{2,1,0:T(8,128)(2,1)S(1)}, bf16[1,8,1792]{2,1,0:T(8,128)(2,1)}, u32[]{:S(2)}) copy-start(bf16[1,8,1792]{2,1,0:T(8,128)(2,1)} %param.15) | copy-start | bytes 86020
  80.2 61.0 %copy-start.17 = (s32[1,3]{1,0:T(1,128)S(1)}, s32[1,3]{1,0:T(1,128)}, u32[]{:S(2)}) copy-start(s32[1,3]{1,0:T(1,128)} %param.17) | copy-start | bytes 40
  140.4 478.7 %copy-start.12 = (bf16[1,3,50,1792]{3,2,1,0:T(8,128)(2,1)S(1)}, bf16[1,3,50,1792]{3,2,1,0:T(8,128)(2,1)}, u32[]{:S(2)}) copy-start(bf16[1,3,50,1792]{3,2,1,0:T(8,128)(2,1)} %param.12) | copy-start | bytes 1612804
  617.7 2.8 copy-start.15
  620.4 1.1 copy-start
  632.8 1.1 copy-start.9
  633.8 0.8 copy-start.4
  636.1 1.3 copy-start.1
  637.5 1.1 copy-start.10
  639.0 1.4 copy-start.5
  639.1 1.3 copy-start.7
  640.4 1.1 copy-start.3
Sparse Core Ops, SparseCore 0:
  635.8 135.9 reduce-scatter.1
where the time goes:
time: 781 us; the launch traced here: 780 us
  blocking collectives  605 us (77%)
  waiting for transfers between devices  128 us (16%)
  between operations  17.2 us (2%)
  local copies, waits for them, and re-layouts  15.5 us (2%)
    psum x1, blocking collectives, body(): total_live = lax.psum(live_here, ('prompt', 'group'))  475 us
    reduce_scatter x1, waiting for transfers between devices, body(): lax.psum_scatter(jnp.concatenate([key_part.reshape(pre_here * lax.axis_si...  128 us
    all_gather x1, blocking collectives, body(): lax.all_gather(prefix_keys, 'group', axis=1, tiled=True)  38.2 us
    psum x1, blocking collectives, body(): reward_sum, reward_sq = lax.psum((reward_sum_here, reward_sq_here), 'group')  29.7 us
    all_gather x1, blocking collectives, body(): lax.all_gather(prefix_values, 'group', axis=1, tiled=True)  28.4 us
    unnamed x1, blocking collectives  27 us
  transfers between devices with their start and end apart: 1, of which 1 were waited for; matrix products, arithmetic and copies ran while one was open for 1% of the time, Pallas kernels for 0%

commit v1 on v0

v1 whole, which is shorter than its diff:
```python
import functools

import math

import jax
import jax.numpy as jnp
from jax import lax
from jax.experimental import pallas as pl
from jax.experimental.pallas import tpu as pltpu
from jax.sharding import PartitionSpec as P

HEAD_DIM = 128
ROWS = 64
MESH = pl.DeviceIdType.MESH
F32 = jnp.float32
BF16 = jnp.bfloat16

masked_score = -1e30
epsilon = 1e-06


def mm(a, b, ca, cb):
    return lax.dot_general(a, b, (((ca,), (cb,)), ((), ())), preferred_element_type=F32)


def bmm(a, b, ca, cb):
    return lax.dot_general(a, b, (((ca,), (cb,)), ((0,), (0,))), preferred_element_type=F32)


def weave(services, pieces):
    done = 0
    for i, service in enumerate(services):
        service()
        upto = 0 if i == 0 else i * len(pieces) // (len(services) - 1)
        while done < upto:
            pieces[done]()
            done += 1


def layer_kernel(
    sizes,
    mask_hbm,
    len_hbm,
    rew_hbm,
    q_hbm,
    ka_hbm,
    va_hbm,
    u_hbm,
    kv_ref,
    gain_ref,
    gq_ref,
    gk_ref,
    gv_ref,
    gpk_ref,
    gpv_ref,
    mask_s,
    len_s,
    rew_s,
    stage,
    qs,
    kas,
    vas,
    gus,
    kvg,
    kpre,
    vpre,
    e_act,
    o_act,
    top_act,
    sum_act,
    beta_s,
    p_pre,
    att,
    gas,
    dsp_s,
    delta_s,
    acc_sq,
    acc_in,
    row_a,
    row_b,
    part,
    r_far,
    r_near,
    meta_z,
    meta_p,
    norm_x,
    in_sem,
    small_sem,
    gf_send,
    gf_recv,
    gn_send,
    gn_recv,
    sf_send,
    sf_recv,
    sn_send,
    sn_recv,
    mz_send,
    mz_recv,
    mp_send,
    mp_recv,
    nx_send,
    nx_recv,
):
    n_prompt, n_group, n_mp, samp, act, heads, pre = sizes
    rows = samp * ROWS
    total_rows = norm_x.shape[2]
    scale = HEAD_DIM ** (-0.5)
    scale2 = scale * math.log2(math.e)
    width_all = heads * HEAD_DIM * n_mp
    half = n_group // 2
    steps = half // 2
    chunks = ((0, heads // 2), (heads // 2, heads))
    n_chunk = len(chunks)
    g = lax.axis_index("group")
    p = lax.axis_index("prompt")
    m = lax.axis_index("mp")

    small = [
        pltpu.make_async_copy(src, dst, small_sem.at[i])
        for i, (src, dst) in enumerate(
            (
                (mask_hbm, mask_s),
                (len_hbm, len_s),
                (rew_hbm, rew_s),
            )
        )
    ]
    for cp in small:
        cp.start()
    loads = [
        pltpu.make_async_copy(src.at[0], stage.at[i], in_sem.at[i])
        for i, src in enumerate((q_hbm, ka_hbm, va_hbm, u_hbm))
    ]
    for cp in loads:
        cp.start()

    barrier = pltpu.get_barrier_semaphore()
    for d in sorted(range(1, n_group), key=lambda d: min(d, n_group - d)):
        pl.semaphore_signal(
            barrier, inc=1, device_id={"group": lax.rem(g + d, n_group)}, device_id_type=MESH
        )
    for d in range(1, n_prompt):
        pl.semaphore_signal(
            barrier, inc=1, device_id={"prompt": lax.rem(p + d, n_prompt)}, device_id_type=MESH
        )
    pl.semaphore_signal(barrier, inc=1, device_id={"mp": 1 - m}, device_id_type=MESH)

    for h in range(heads):
        cols = slice(h * HEAD_DIM, (h + 1) * HEAD_DIM)
        slab = jnp.concatenate(
            [kv_ref[0, :, cols].astype(F32), kv_ref[1, :, cols].astype(F32)], axis=0
        )
        kvg[g, h] = slab.astype(BF16)

    pl.semaphore_wait(barrier, n_group + n_prompt - 1)

    def remote(src, dst, send, recv, where):
        return pltpu.make_async_remote_copy(
            src_ref=src,
            dst_ref=dst,
            send_sem=send,
            recv_sem=recv,
            device_id=where,
            device_id_type=MESH,
        )

    def heads_of(k):
        lo, hi = chunks[k]
        return pl.ds(lo, hi - lo)

    def away(way, dist):
        return lax.rem(g + (dist if way == 0 else n_group - dist), n_group)

    def behind(way, dist):
        return away(1 - way, dist)

    def gather_far(way, s, k):
        ref = kvg.at[behind(way, 2 * s), heads_of(k)]
        to = {"group": away(way, 2)}
        return remote(ref, ref, gf_send.at[way, s, k], gf_recv.at[way, s, k], to)

    def gather_near(way, s, k):
        ref = kvg.at[behind(way, 2 * s), heads_of(k)]
        to = {"group": away(way, 1)}
        return remote(ref, ref, gn_send.at[way, s, k], gn_recv.at[way, s, k], to)

    def has_far(way, s, k):
        return way == k or s < steps - 1

    def gather_service(s, k):
        for way in (k, 1 - k):
            if s > 0 and has_far(way, s - 1, k):
                gather_far(way, s - 1, k).wait_recv()
            if s < steps and has_far(way, s, k):
                gather_far(way, s, k).start()
            if s < steps:
                gather_near(way, s, k).start()
        if s == steps:
            for way in range(2):
                for t in range(steps):
                    gather_near(way, t, k).wait_recv()

    def meta_group(d):
        return remote(
            meta_z.at[g],
            meta_z.at[g],
            mz_send.at[d],
            mz_recv.at[d],
            {"group": lax.rem(g + d, n_group)},
        )

    def meta_prompt(d):
        return remote(
            meta_p.at[0],
            meta_p.at[d],
            mp_send.at[d],
            mp_recv.at[d],
            {"prompt": lax.rem(p + d, n_prompt)},
        )


    def unpack(i, dst, gain, lo, hi):
        pad = jnp.zeros((16, HEAD_DIM), dst.dtype)
        for h in range(lo, hi):
            cols = slice(h * HEAD_DIM, (h + 1) * HEAD_DIM)
            for s in range(samp):
                block = stage[i, s, :, cols]
                if gain:
                    block = block.astype(F32) * gain_ref[cols].astype(F32).reshape(1, HEAD_DIM)
                dst[h, s * ROWS + ROWS - 16 : (s + 1) * ROWS] = pad
                dst[h, s * ROWS : s * ROWS + act] = block

    def unpack_first(i, dst, gain):
        loads[i].wait()
        unpack(i, dst, gain, 0, heads // 2)

    def unpack_rest(i, dst, gain):
        unpack(i, dst, gain, heads // 2, heads)

    causal = (
        lax.broadcasted_iota(jnp.int32, (ROWS, ROWS), 0)
        >= lax.broadcasted_iota(jnp.int32, (ROWS, ROWS), 1)
    )

    def three(x):
        return x.reshape(samp, ROWS, x.shape[-1])

    def flat(x):
        return x.reshape(rows, x.shape[-1])

    def own_part(hs):
        raw = [bmm(three(qs[h]), three(kas[h]), 2, 2) for h in hs]
        held = []
        for h, sc in zip(hs, raw):
            sc = flat(jnp.where(causal[None], sc, masked_score))
            top = jnp.max(sc, axis=1, keepdims=True)
            top_act[h] = top
            held.append(jnp.exp2((sc - top) * scale2))
        outs = [bmm(three(ea.astype(BF16)), three(vas[h]), 2, 1) for h, ea in zip(hs, held)]
        for h, ea, out in zip(hs, held, outs):
            e_act[h] = ea
            sum_act[h] = jnp.sum(ea, axis=1, keepdims=True)
            o_act[h] = flat(out)

    def meta_send():
        for cp in small:
            cp.wait()
        lane = lax.broadcasted_iota(jnp.int32, (1, 128), 1)
        mask_row = jnp.zeros((1, 128), F32)
        for i in range(pre):
            mask_row = jnp.where(lane == g * pre + i, mask_s[0, i].astype(F32), mask_row)
        live_here = len_s[0, 0]
        rsum_here = rew_s[0, 0]
        rsq_here = rew_s[0, 0] * rew_s[0, 0]
        for s in range(1, samp):
            live_here = live_here + len_s[0, s]
            rsum_here = rsum_here + rew_s[0, s]
            rsq_here = rsq_here + rew_s[0, s] * rew_s[0, s]
        sum_row = jnp.where(
            lane == 0,
            live_here.astype(F32),
            jnp.where(
                lane == 1,
                rsum_here.astype(F32),
                jnp.where(lane == 2, rsq_here.astype(F32), 0.0),
            ),
        )
        meta_z[g] = jnp.concatenate([mask_row, sum_row], axis=1)
        for d in range(1, n_group):
            meta_group(d).start()

    def meta_sum():
        for d in range(1, n_group):
            meta_group(d).wait_recv()
        total = meta_z[0]
        for d in range(1, n_group):
            total = total + meta_z[d]
        meta_p[0] = total
        for d in range(1, n_prompt):
            meta_prompt(d).start()

    pieces = [
        meta_send,
        functools.partial(unpack_first, 0, qs, False),
        functools.partial(unpack_rest, 0, qs, False),
        functools.partial(unpack_first, 1, kas, False),
        functools.partial(unpack_rest, 1, kas, False),
        functools.partial(unpack_first, 2, vas, False),
        functools.partial(unpack_rest, 2, vas, False),
        functools.partial(unpack_first, 3, gus, True),
        functools.partial(unpack_rest, 3, gus, True),
        meta_sum,
    ]
    trios = [list(range(h, min(h + 3, heads))) for h in range(0, heads, 3)]
    pieces += [functools.partial(own_part, hs) for hs in trios]
    services = [
        functools.partial(gather_service, s, k) for s in range(steps) for k in range(n_chunk)
    ]
    weave(services, pieces)

    mask_all = meta_p[0][:, : pre * n_group]
    sums = meta_p[0][:, 128:]

    def forward_scores(h):
        blk = kvg[:, h].astype(F32)
        keys = blk[:, :8].reshape(pre * n_group, HEAD_DIM).astype(BF16)
        vals = blk[:, 8:].reshape(pre * n_group, HEAD_DIM).astype(BF16)
        kpre[h] = keys
        vpre[h] = vals
        return mm(qs[h], keys, 1, 1)

    def forward_probs(h, sp):
        sp = jnp.where(mask_all > 0.5, sp, masked_score)
        ta = top_act[h]
        top = jnp.maximum(jnp.max(sp, axis=1, keepdims=True), ta)
        ep = jnp.exp2((sp - top) * scale2)
        alpha = jnp.exp2((ta - top) * scale2)
        inv = 1.0 / (jnp.sum(ep, axis=1, keepdims=True) + alpha * sum_act[h])
        pp = (ep * inv).astype(BF16)
        p_pre[h] = pp
        beta = alpha * inv
        beta_s[h] = beta
        return pp, beta

    def forward_values(h, pp, beta):
        return mm(pp, vpre[h], 1, 0) + beta * o_act[h]

    def forward_sums(h, at):
        att[h] = at
        if h == 0:
            acc_sq[...] = at * at
            acc_in[...] = at * gus[h]
        else:
            acc_sq[...] += at * at
            acc_in[...] += at * gus[h]

    def forward(lo, hi):
        held = {}
        for i in range(lo, hi + 3):
            if i < hi:
                held["s", i] = forward_scores(i)
            if lo <= i - 1 < hi:
                held["p", i - 1] = forward_probs(i - 1, held.pop(("s", i - 1)))
            if lo <= i - 2 < hi:
                held["a", i - 2] = forward_values(i - 2, *held.pop(("p", i - 2)))
            if lo <= i - 3 < hi:
                forward_sums(i - 3, held.pop(("a", i - 3)))

    for k in range(n_chunk):
        gather_service(steps, k)
        forward(*chunks[k])

    col_sq = jnp.sum(acc_sq[...], axis=1, keepdims=True)
    col_in = jnp.sum(acc_in[...], axis=1, keepdims=True)
    lanes = lax.broadcasted_iota(jnp.int32, (rows, 128), 1)
    both = jnp.where(lanes == 0, col_sq, jnp.where(lanes == 1, col_in, 0.0))
    both = jnp.concatenate([both, jnp.zeros((total_rows - rows, 128), F32)], axis=0)
    norm_x[0] = both.T[:8]
    swap = remote(norm_x.at[0], norm_x.at[1], nx_send, nx_recv, {"mp": 1 - m})
    swap.start()

    for d in range(1, n_prompt):
        meta_prompt(d).wait_recv()
    live_all = meta_p[0]
    for d in range(1, n_prompt):
        live_all = live_all + meta_p[d]
    n_samp = samp * n_group
    loss_scale = (n_prompt * n_samp * act) / live_all[:, 128:129]
    rsum = sums[:, 1:2]
    rsq = sums[:, 2:3]
    spread = jnp.sqrt(n_samp * rsq - rsum * rsum) / n_samp
    tok = lax.broadcasted_iota(jnp.int32, (ROWS, 1), 0)
    weights = []
    for s in range(samp):
        adv = (rew_s[0, s].astype(F32) - rsum / n_samp) / (spread + 1.0)
        adv = jnp.broadcast_to(adv * loss_scale, (ROWS, 1))
        weights.append(jnp.where(tok < len_s[0, s], adv, 0.0))
    weight = jnp.concatenate(weights, axis=0)

    swap.wait_recv()
    summed = norm_x[0] + norm_x[1]
    summed = jnp.concatenate([summed, jnp.zeros((120, total_rows), F32)], axis=0)
    summed = summed.T
    squares = summed[:rows, 0:1]
    inner = summed[:rows, 1:2] * weight
    inverse = lax.rsqrt(squares / width_all + epsilon)
    factor = inverse * inverse * inner / width_all
    row_a[...] = jnp.broadcast_to(inverse * weight, row_a.shape)
    row_b[...] = jnp.broadcast_to(inverse * factor, row_b.shape)

    def back_grad(h):
        at = att[h]
        gb = (row_a[...] * gus[h] - row_b[...] * at).astype(BF16)
        gas[h] = gb
        delta = jnp.sum(gb.astype(F32) * at, axis=1, keepdims=True)
        delta_s[h] = delta
        return gb, delta, mm(gb, vpre[h], 1, 1)

    def back_scores(h, gb, delta, dp):
        pp = p_pre[h]
        ds = (pp.astype(F32) * (dp - delta)).astype(BF16)
        dsp_s[h] = ds
        return mm(ds, qs[h], 0, 0), mm(pp, gb, 0, 0)

    def back_part(h, pk, pv):
        slab = jnp.concatenate(
            [
                (pk * scale).reshape(n_group, pre, HEAD_DIM),
                pv.reshape(n_group, pre, HEAD_DIM),
            ],
            axis=1,
        )
        part[:, h] = slab.astype(BF16)

    def backward_prefix(lo, hi):
        held = {}
        for i in range(lo, hi + 2):
            if i < hi:
                held["d", i] = back_grad(i)
            if lo <= i - 1 < hi:
                held["s", i - 1] = back_scores(i - 1, *held.pop(("d", i - 1)))
            if lo <= i - 2 < hi:
                back_part(i - 2, *held.pop(("s", i - 2)))

    def backward_own(hs):
        grads = [three(gas[h]) for h in hs]
        probs = [three((e_act[h] * beta_s[h]).astype(BF16)) for h in hs]
        dps = [bmm(gb, three(vas[h]), 2, 2) for h, gb in zip(hs, grads)]
        gvs = [bmm(pa, gb, 1, 1) for pa, gb in zip(probs, grads)]
        gqs = [mm(dsp_s[h], kpre[h], 1, 0) for h in hs]
        dss = [
            (pa.astype(F32) * (dp - three(delta_s[h]))).astype(BF16)
            for h, pa, dp in zip(hs, probs, dps)
        ]
        gqs = [
            (three(gq) + bmm(ds, three(kas[h]), 2, 1)) * scale
            for h, gq, ds in zip(hs, gqs, dss)
        ]
        gks = [bmm(ds, three(qs[h]), 1, 1) * scale for h, ds in zip(hs, dss)]
        for dst, vals in ((gv_ref, gvs), (gq_ref, gqs), (gk_ref, gks)):
            for h, val in zip(hs, vals):
                cols = slice(h * HEAD_DIM, (h + 1) * HEAD_DIM)
                for s in range(samp):
                    dst[0, s, :, cols] = val[s, :act].astype(BF16)

    def block(way, dist):
        return away(way, dist)

    def reduce_far(way, s, k):
        src = part.at[block(way, half - 2 * s), heads_of(k)]
        dst = r_far.at[way, s, heads_of(k)]
        to = {"group": away(way, 2)}
        return remote(src, dst, sf_send.at[way, s, k], sf_recv.at[way, s, k], to)

    def reduce_near(way, s, k):
        src = part.at[block(way, half - 1 - 2 * s), heads_of(k)]
        dst = r_near.at[way, s, heads_of(k)]
        to = {"group": away(way, 1)}
        return remote(src, dst, sn_send.at[way, s, k], sn_recv.at[way, s, k], to)

    def sends_far(way, s, k):
        return way == k or s > 0

    def arrived(way, s, k):
        lo, hi = chunks[k]
        reduce_near(way, s - 1, k).wait_recv()
        got = r_near[way, s - 1, lo:hi].astype(F32)
        if sends_far(way, s - 1, k):
            reduce_far(way, s - 1, k).wait_recv()
            got = got + r_far[way, s - 1, lo:hi].astype(F32)
        return got

    def reduce_service(s, k):
        lo, hi = chunks[k]
        for way in (k, 1 - k):
            if sends_far(way, s, k):
                if s > 0:
                    at = block(way, half - 2 * s)
                    here = part[at, lo:hi].astype(F32) + arrived(way, s, k)
                    part[at, lo:hi] = here.astype(BF16)
                reduce_far(way, s, k).start()
        for way in (k, 1 - k):
            reduce_near(way, s, k).start()

    def reduce_last(k):
        lo, hi = chunks[k]
        tot = part[g, lo:hi].astype(F32)
        for way in range(2):
            tot = tot + arrived(way, steps, k)
        for h in range(lo, hi):
            cols = slice(h * HEAD_DIM, (h + 1) * HEAD_DIM)
            gpk_ref[0, :, cols] = tot[h - lo, :8].astype(BF16)
            gpv_ref[0, :, cols] = tot[h - lo, 8:].astype(BF16)

    def serve(s, k):
        return functools.partial(reduce_service, s, k)

    (lo0, hi0), (lo1, hi1) = chunks
    backward_prefix(lo0, hi0)
    reduce_service(0, 0)
    backward_prefix(lo1, hi1)
    services = [serve(0, 1)] + [serve(s, k) for s in range(1, steps) for k in range(n_chunk)]
    weave(services + [lambda: None], [functools.partial(backward_own, hs) for hs in trios])
    for k in range(n_chunk):
        reduce_last(k)

    for d in range(1, n_group):
        meta_group(d).wait_send()
    for d in range(1, n_prompt):
        meta_prompt(d).wait_send()
    swap.wait_send()

    for k in range(n_chunk):
        for way in range(2):
            for s in range(steps):
                if has_far(way, s, k):
                    gather_far(way, s, k).wait_send()
                gather_near(way, s, k).wait_send()
                if sends_far(way, s, k):
                    reduce_far(way, s, k).wait_send()
                reduce_near(way, s, k).wait_send()


def store_kernel(*refs):
    n = (len(refs) - 1) // 2
    sems = refs[-1]
    copies = [pltpu.make_async_copy(refs[i], refs[n + i], sems.at[i]) for i in range(n)]
    for cp in copies:
        cp.start()
    for cp in copies:
        cp.wait()


def body(q, ka, va, u, kp, vp, mask, lengths, rewards, gain):
    _, samp, act, width = q.shape
    heads = width // HEAD_DIM
    pre = kp.shape[1]
    n_prompt, n_group, n_mp = (lax.axis_size(a) for a in ("prompt", "group", "mp"))
    rows = samp * ROWS
    total_rows = -(-rows // 128) * 128
    half = n_group // 2
    steps = half // 2
    n_chunk = 2
    hbm = pl.BlockSpec(memory_space=pltpu.HBM)
    vmem = pl.BlockSpec(memory_space=pltpu.VMEM)
    big = jax.ShapeDtypeStruct(q.shape, BF16)
    small = jax.ShapeDtypeStruct(kp.shape, BF16)
    dma = pltpu.SemaphoreType.DMA
    v = pltpu.VMEM
    kv = jnp.concatenate([kp, vp], axis=0)
    sizes = (n_prompt, n_group, n_mp, samp, act, heads, pre)
    slab = (heads, 2 * pre, HEAD_DIM)
    results = pl.pallas_call(
        functools.partial(layer_kernel, sizes),
        out_shape=(big, big, big, small, small),
        in_specs=[hbm] * 7 + [vmem] * 2,
        out_specs=[vmem] * 5,
        scratch_shapes=[
            pltpu.SMEM(mask.shape, jnp.int32),
            pltpu.SMEM(lengths.shape, jnp.int32),
            pltpu.SMEM(rewards.shape, jnp.int32),
            v((4, samp, act, width), BF16),
            v((heads, rows, HEAD_DIM), BF16),
            v((heads, rows, HEAD_DIM), BF16),
            v((heads, rows, HEAD_DIM), BF16),
            v((heads, rows, HEAD_DIM), F32),
            v((n_group,) + slab, BF16),
            v((heads, pre * n_group, HEAD_DIM), BF16),
            v((heads, pre * n_group, HEAD_DIM), BF16),
            v((heads, rows, ROWS), F32),
            v((heads, rows, HEAD_DIM), F32),
            v((heads, rows, 1), F32),
            v((heads, rows, 1), F32),
            v((heads, rows, 1), F32),
            v((heads, rows, pre * n_group), BF16),
            v((heads, rows, HEAD_DIM), F32),
            v((heads, rows, HEAD_DIM), BF16),
            v((heads, rows, pre * n_group), BF16),
            v((heads, rows, 1), F32),
            v((rows, HEAD_DIM), F32),
            v((rows, HEAD_DIM), F32),
            v((rows, HEAD_DIM), F32),
            v((rows, HEAD_DIM), F32),
            v((n_group,) + slab, BF16),
            v((2, steps) + slab, BF16),
            v((2, steps) + slab, BF16),
            v((n_group, 1, 256), F32),
            v((n_prompt, 1, 256), F32),
            v((2, 8, total_rows), F32),
            dma((4,)),
            dma((3,)),
            dma((2, steps, n_chunk)),
            dma((2, steps, n_chunk)),
            dma((2, steps, n_chunk)),
            dma((2, steps, n_chunk)),
            dma((2, steps, n_chunk)),
            dma((2, steps, n_chunk)),
            dma((2, steps, n_chunk)),
            dma((2, steps, n_chunk)),
            dma((n_group,)),
            dma((n_group,)),
            dma((n_prompt,)),
            dma((n_prompt,)),
            dma(()),
            dma(()),
        ],
        compiler_params=pltpu.CompilerParams(
            collective_id=0, has_side_effects=True, vmem_limit_bytes=52 * 1024 * 1024
        ),
    )(mask, lengths, rewards, q, ka, va, u, kv, gain)
    return pl.pallas_call(
        store_kernel,
        out_shape=(big, big, big, small, small),
        in_specs=[pl.BlockSpec(memory_space=pl.ANY)] * 5,
        out_specs=[hbm] * 5,
        scratch_shapes=[dma((5,))],
        compiler_params=pltpu.CompilerParams(vmem_limit_bytes=4 * 1024 * 1024),
    )(*results)


def solution(mesh):
    big = P("prompt", "group", None, "mp")
    mid = P("prompt", "group", "mp")
    small = P("prompt", "group")
    return jax.shard_map(
        body,
        mesh=mesh,
        in_specs=(big, big, big, big, mid, mid, small, small, small, P("mp")),
        out_specs=(big, big, big, mid, mid),
        check_vma=False,
    )
```

time: 781 us -> 65.1 us (0.08)
  blocking collectives: 605 us -> 0 us
  waiting for transfers between devices: 128 us -> 0 us
  Pallas kernels: 0 us -> 63.4 us
  between operations: 17.2 us -> 0.7 us
  local copies, waits for them, and re-layouts: 15.5 us -> 0.02 us
    psum x3 -> x0, blocking collectives: 511 us -> none  [the longest x1 475 us: body(): total_live = lax.psum(live_here, ('prompt', 'group'))]
    reduce_scatter x1 -> x0, waiting for transfers between devices: 128 us -> none  [body(): lax.psum_scatter(jnp.concatenate([key_part.reshape(pre_here * lax.axis_si...]
    all_gather x2 -> x0, blocking collectives: 66.6 us -> none  [the longest x1 38.2 us: body(): lax.all_gather(prefix_keys, 'group', axis=1, tiled=True)]
    pallas_call x0 -> x2, Pallas kernels: none -> 63.4 us  [the longest x1 62.2 us: body(): pl.pallas_call(functools.partial(layer_kernel, sizes), out_shape=(big, bi...]
    unnamed x1 -> x0, blocking collectives: 27 us -> none
  transfers between devices with their start and end apart: 1 -> 0, of which waited for: 1 -> 0; matrix products, arithmetic and copies ran while one was open for 1% -> 0% of each run, Pallas kernels for 0% -> 0%
where the time goes in v1:
time: 65.1 us; the launch traced here: 65 us
  Pallas kernels  63.4 us (97%)
  other arithmetic  0.79 us (1%)
  between operations  0.7 us (1%)
    pallas_call x1, Pallas kernels, body(): pl.pallas_call(functools.partial(layer_kernel, sizes), out_shape=(big, bi...  62.2 us

profile of v1, /device:TPU:24, one launch (start us, length us, event | category | flops | bytes accessed | tf_op | source)
XLA Modules:
  0.0 65.0 jit_solution(11967476153402962491)
XLA Ops:
  0.6 0.0 copy-start
  0.6 0.0 copy-start.3
  0.7 0.0 copy-start.2
  0.7 0.0 copy-start.1
  0.7 0.8 %pad_maximum_fusion.kv_ref = bf16[2,8,1792]{2,1,0:T(8,128)(2,1)S(1)} fusion(bf16[1,8,1792]{2,1,0:T(8,128)(2,1)} %param.15, bf16[1,8,1792]{2,1,0:T(8,128)(2,1)} %param.14), kind=kLoop, calls=%fused_computation | loop fusion | flops 28672 | bytes 114688 | tf_op jit(solution)/shard_map/concatenate | solution.py:570
  1.5 0.0 copy-done
  1.5 0.0 copy-done.3
  1.5 0.0 copy-done.2
  1.5 0.0 copy-done.1
  1.5 62.2 %shard_map.137 = (bf16[1,3,50,1792]{3,2,1,0:T(8,128)(2,1)S(1)}, bf16[1,3,50,1792]{3,2,1,0:T(8,128)(2,1)S(1)}, bf16[1,3,50,1792]{3,2,1,0:T(8,128)(2,1)S(1)}, bf16...) custom-call(s32[1,8]{1,0:T(1,128)S(1)} %copy-done.1, s32[1,3]{1,0:T(1,128)S(1)} %copy-done.2, s32[1,3]{1,0:T(1,128)S(1)} %copy-done.3, ...), custom_call_target="tpu_custom_call" | custom-call | tf_op jit(solution)/shard_map/pallas_call | solution.py:573
  63.7 1.3 %shard_map.138 = (bf16[1,3,50,1792]{3,2,1,0:T(8,128)(2,1)}, bf16[1,3,50,1792]{3,2,1,0:T(8,128)(2,1)}, bf16[1,3,50,1792]{3,2,1,0:T(8,128)(2,1)}, bf16[1,8,1792]{2,1,0:T(8,128)(2,1)}, bf16[1,8,1792]{2,1,0:T(8,128)(2,1)}) custom-call(bf16[1,3,50,1792]{3,2,1,0:T(8,128)(2,1)S(1)} %get-tuple-element.10.refs_0_, ...), custom_call_target="tpu_custom_call" | custom-call | tf_op jit(solution)/shard_map/pallas_call | solution.py:631
Async XLA Ops:
  0.6 0.8 %copy-start = (bf16[1792]{0:T(1024)(128)(2,1)S(1)}, bf16[1792]{0:T(1024)(128)(2,1)}, u32[]{:S(2)}) copy-start(bf16[1792]{0:T(1024)(128)(2,1)} %gain_ref.1) | copy-start | bytes 10756
  0.6 0.8 %copy-start.3 = (s32[1,3]{1,0:T(1,128)S(1)}, s32[1,3]{1,0:T(1,128)}, u32[]{:S(2)}) copy-start(s32[1,3]{1,0:T(1,128)} %rew_hbm.1) | copy-start | bytes 40
  0.7 0.8 %copy-start.2 = (s32[1,3]{1,0:T(1,128)S(1)}, s32[1,3]{1,0:T(1,128)}, u32[]{:S(2)}) copy-start(s32[1,3]{1,0:T(1,128)} %len_hbm.1) | copy-start | bytes 40
  0.7 0.8 %copy-start.1 = (s32[1,8]{1,0:T(1,128)S(1)}, s32[1,8]{1,0:T(1,128)}, u32[]{:S(2)}) copy-start(s32[1,8]{1,0:T(1,128)} %mask_hbm.1) | copy-start | bytes 100

commit v2 on v1

--- a/solution.py
+++ b/solution.py
@@ -31,7 +31,7 @@
     done = 0
     for i, service in enumerate(services):
         service()
-        upto = 0 if i == 0 else i * len(pieces) // (len(services) - 1)
+        upto = -(-(i + 1) * len(pieces) // len(services))
         while done < upto:
             pieces[done]()
             done += 1
@@ -187,18 +187,22 @@
     def has_far(way, s, k):
         return way == k or s < steps - 1
 
-    def gather_service(s, k):
-        for way in (k, 1 - k):
-            if s > 0 and has_far(way, s - 1, k):
-                gather_far(way, s - 1, k).wait_recv()
-            if s < steps and has_far(way, s, k):
-                gather_far(way, s, k).start()
-            if s < steps:
+    def gather_step(s):
+        for k in range(n_chunk):
+            for way in (k, 1 - k):
+                if s > 0:
+                    gather_far(way, s - 1, k).wait_recv()
+                if has_far(way, s, k):
+                    gather_far(way, s, k).start()
+        for k in range(n_chunk):
+            for way in (k, 1 - k):
                 gather_near(way, s, k).start()
-        if s == steps:
-            for way in range(2):
-                for t in range(steps):
-                    gather_near(way, t, k).wait_recv()
+
+    def gather_last(k):
+        gather_far(k, steps - 1, k).wait_recv()
+        for way in range(2):
+            for t in range(steps):
+                gather_near(way, t, k).wait_recv()
 
     def meta_group(d):
         return remote(
@@ -313,10 +317,7 @@
     ]
     trios = [list(range(h, min(h + 3, heads))) for h in range(0, heads, 3)]
     pieces += [functools.partial(own_part, hs) for hs in trios]
-    services = [
-        functools.partial(gather_service, s, k) for s in range(steps) for k in range(n_chunk)
-    ]
-    weave(services, pieces)
+    weave([functools.partial(gather_step, s) for s in range(steps)], pieces)
 
     mask_all = meta_p[0][:, : pre * n_group]
     sums = meta_p[0][:, 128:]
@@ -367,7 +368,7 @@
                 forward_sums(i - 3, held.pop(("a", i - 3)))
 
     for k in range(n_chunk):
-        gather_service(steps, k)
+        gather_last(k)
         forward(*chunks[k])
 
     col_sq = jnp.sum(acc_sq[...], axis=1, keepdims=True)
@@ -490,7 +491,11 @@
             got = got + r_far[way, s - 1, lo:hi].astype(F32)
         return got
 
-    def reduce_service(s, k):
+    def start_near(s, k):
+        for way in (k, 1 - k):
+            reduce_near(way, s, k).start()
+
+    def reduce_on(s, k):
         lo, hi = chunks[k]
         for way in (k, 1 - k):
             if sends_far(way, s, k):
@@ -499,8 +504,14 @@
                     here = part[at, lo:hi].astype(F32) + arrived(way, s, k)
                     part[at, lo:hi] = here.astype(BF16)
                 reduce_far(way, s, k).start()
-        for way in (k, 1 - k):
-            reduce_near(way, s, k).start()
+
+    def reduce_step(s):
+        for k in range(n_chunk):
+            if s > 0:
+                reduce_on(s, k)
+        if s + 1 < steps:
+            for k in range(n_chunk):
+                start_near(s + 1, k)
 
     def reduce_last(k):
         lo, hi = chunks[k]
@@ -512,15 +523,14 @@
             gpk_ref[0, :, cols] = tot[h - lo, :8].astype(BF16)
             gpv_ref[0, :, cols] = tot[h - lo, 8:].astype(BF16)
 
-    def serve(s, k):
-        return functools.partial(reduce_service, s, k)
-
-    (lo0, hi0), (lo1, hi1) = chunks
-    backward_prefix(lo0, hi0)
-    reduce_service(0, 0)
-    backward_prefix(lo1, hi1)
-    services = [serve(0, 1)] + [serve(s, k) for s in range(1, steps) for k in range(n_chunk)]
-    weave(services + [lambda: None], [functools.partial(backward_own, hs) for hs in trios])
+    for k in range(n_chunk):
+        backward_prefix(*chunks[k])
+        reduce_on(0, k)
+        start_near(0, k)
+    weave(
+        [functools.partial(reduce_step, s) for s in range(steps)],
+        [functools.partial(backward_own, hs) for hs in trios],
+    )
     for k in range(n_chunk):
         reduce_last(k)
 

time: 65.1 us -> 65.2 us (level); the launches traced: 65 us -> 64.1 us
  Pallas kernels: 63.4 us -> 62.6 us
    pallas_call x1, Pallas kernels: 62.2 us -> 61.3 us  [body(): pl.pallas_call(functools.partial(layer_kernel, sizes), out_shape=(big, bi...]
where the time goes in v2:
time: 65.2 us; the launch traced here: 64.1 us
  Pallas kernels  62.6 us (96%)
  other arithmetic  0.79 us (1%)
  between operations  0.7 us (1%)
    pallas_call x1, Pallas kernels, body(): pl.pallas_call(functools.partial(layer_kernel, sizes), out_shape=(big, bi...  61.3 us

profile of v2, /device:TPU:24, one launch (start us, length us, event | category | flops | bytes accessed | tf_op | source)
XLA Modules:
  0.0 64.1 jit_solution(15031968731004074872)
XLA Ops:
  0.6 0.0 copy-start
  0.6 0.0 copy-start.3
  0.7 0.0 copy-start.2
  0.7 0.0 copy-start.1
  0.7 0.8 %pad_maximum_fusion.kv_ref = bf16[2,8,1792]{2,1,0:T(8,128)(2,1)S(1)} fusion(bf16[1,8,1792]{2,1,0:T(8,128)(2,1)} %param.15, bf16[1,8,1792]{2,1,0:T(8,128)(2,1)} %param.14), kind=kLoop, calls=%fused_computation | loop fusion | flops 28672 | bytes 114688 | tf_op jit(solution)/shard_map/concatenate | solution.py:580
  1.5 0.0 copy-done
  1.5 0.0 copy-done.3
  1.5 0.0 copy-done.2
  1.5 0.0 copy-done.1
  1.5 61.3 %shard_map.137 = (bf16[1,3,50,1792]{3,2,1,0:T(8,128)(2,1)S(1)}, bf16[1,3,50,1792]{3,2,1,0:T(8,128)(2,1)S(1)}, bf16[1,3,50,1792]{3,2,1,0:T(8,128)(2,1)S(1)}, bf16...) custom-call(s32[1,8]{1,0:T(1,128)S(1)} %copy-done.1, s32[1,3]{1,0:T(1,128)S(1)} %copy-done.2, s32[1,3]{1,0:T(1,128)S(1)} %copy-done.3, ...), custom_call_target="tpu_custom_call" | custom-call | tf_op jit(solution)/shard_map/pallas_call | solution.py:583
  62.8 1.3 %shard_map.138 = (bf16[1,3,50,1792]{3,2,1,0:T(8,128)(2,1)}, bf16[1,3,50,1792]{3,2,1,0:T(8,128)(2,1)}, bf16[1,3,50,1792]{3,2,1,0:T(8,128)(2,1)}, bf16[1,8,1792]{2,1,0:T(8,128)(2,1)}, bf16[1,8,1792]{2,1,0:T(8,128)(2,1)}) custom-call(bf16[1,3,50,1792]{3,2,1,0:T(8,128)(2,1)S(1)} %get-tuple-element.10.refs_0_, ...), custom_call_target="tpu_custom_call" | custom-call | tf_op jit(solution)/shard_map/pallas_call | solution.py:641
Async XLA Ops:
  0.6 0.8 %copy-start = (bf16[1792]{0:T(1024)(128)(2,1)S(1)}, bf16[1792]{0:T(1024)(128)(2,1)}, u32[]{:S(2)}) copy-start(bf16[1792]{0:T(1024)(128)(2,1)} %gain_ref.1) | copy-start | bytes 10756
  0.6 0.8 %copy-start.3 = (s32[1,3]{1,0:T(1,128)S(1)}, s32[1,3]{1,0:T(1,128)}, u32[]{:S(2)}) copy-start(s32[1,3]{1,0:T(1,128)} %rew_hbm.1) | copy-start | bytes 40
  0.7 0.8 %copy-start.2 = (s32[1,3]{1,0:T(1,128)S(1)}, s32[1,3]{1,0:T(1,128)}, u32[]{:S(2)}) copy-start(s32[1,3]{1,0:T(1,128)} %len_hbm.1) | copy-start | bytes 40
  0.7 0.8 %copy-start.1 = (s32[1,8]{1,0:T(1,128)S(1)}, s32[1,8]{1,0:T(1,128)}, u32[]{:S(2)}) copy-start(s32[1,8]{1,0:T(1,128)} %mask_hbm.1) | copy-start | bytes 100

commit v3 on v2

--- a/solution.py
+++ b/solution.py
@@ -79,21 +79,16 @@
     row_a,
     row_b,
     part,
-    r_far,
-    r_near,
+    r_in,
     meta_z,
     meta_p,
     norm_x,
     in_sem,
     small_sem,
-    gf_send,
-    gf_recv,
-    gn_send,
-    gn_recv,
-    sf_send,
-    sf_recv,
-    sn_send,
-    sn_recv,
+    g_send,
+    g_recv,
+    s_send,
+    s_recv,
     mz_send,
     mz_recv,
     mp_send,
@@ -108,12 +103,20 @@
     scale2 = scale * math.log2(math.e)
     width_all = heads * HEAD_DIM * n_mp
     half = n_group // 2
-    steps = half // 2
     chunks = ((0, heads // 2), (heads // 2, heads))
     n_chunk = len(chunks)
     g = lax.axis_index("group")
     p = lax.axis_index("prompt")
     m = lax.axis_index("mp")
+    core = lax.rem(p, 2)
+
+    def by_core(f, *args):
+        for mine, stride in ((0, 3), (1, 2)):
+
+            @pl.when(core == mine)
+            def _(stride=stride):
+                f(stride, *args)
+
 
     small = [
         pltpu.make_async_copy(src, dst, small_sem.at[i])
@@ -168,41 +171,43 @@
         lo, hi = chunks[k]
         return pl.ds(lo, hi - lo)
 
+    def reach(way, k):
+        return half if way == k else half - 1
+
+    def ways_of(k):
+        return (k, 1 - k)
+
     def away(way, dist):
         return lax.rem(g + (dist if way == 0 else n_group - dist), n_group)
 
     def behind(way, dist):
         return away(1 - way, dist)
 
-    def gather_far(way, s, k):
-        ref = kvg.at[behind(way, 2 * s), heads_of(k)]
-        to = {"group": away(way, 2)}
-        return remote(ref, ref, gf_send.at[way, s, k], gf_recv.at[way, s, k], to)
-
-    def gather_near(way, s, k):
-        ref = kvg.at[behind(way, 2 * s), heads_of(k)]
-        to = {"group": away(way, 1)}
-        return remote(ref, ref, gn_send.at[way, s, k], gn_recv.at[way, s, k], to)
-
-    def has_far(way, s, k):
-        return way == k or s < steps - 1
-
-    def gather_step(s):
+    def gather_copy(stride, way, dist, k):
+        held = (dist - 1) // stride * stride
+        ref = kvg.at[behind(way, held), heads_of(k)]
+        at = (way, dist - 1, k)
+        return remote(ref, ref, g_send.at[at], g_recv.at[at], {"group": away(way, dist - held)})
+
+    def gather_step(stride, s):
+        held = stride * s
         for k in range(n_chunk):
-            for way in (k, 1 - k):
-                if s > 0:
-                    gather_far(way, s - 1, k).wait_recv()
-                if has_far(way, s, k):
-                    gather_far(way, s, k).start()
+            for way in ways_of(k):
+                if 0 < held < reach(way, k):
+                    gather_copy(stride, way, held, k).wait_recv()
+                if held + stride <= reach(way, k):
+                    gather_copy(stride, way, held + stride, k).start()
         for k in range(n_chunk):
-            for way in (k, 1 - k):
-                gather_near(way, s, k).start()
-
-    def gather_last(k):
-        gather_far(k, steps - 1, k).wait_recv()
-        for way in range(2):
-            for t in range(steps):
-                gather_near(way, t, k).wait_recv()
+            for dist in range(held + stride - 1, held, -1):
+                for way in ways_of(k):
+                    if dist <= reach(way, k):
+                        gather_copy(stride, way, dist, k).start()
+
+    def gather_last(stride, k):
+        for way in ways_of(k):
+            for dist in range(1, reach(way, k) + 1):
+                if dist % stride or dist == reach(way, k):
+                    gather_copy(stride, way, dist, k).wait_recv()
 
     def meta_group(d):
         return remote(
@@ -317,7 +322,7 @@
     ]
     trios = [list(range(h, min(h + 3, heads))) for h in range(0, heads, 3)]
     pieces += [functools.partial(own_part, hs) for hs in trios]
-    weave([functools.partial(gather_step, s) for s in range(steps)], pieces)
+    weave([functools.partial(by_core, gather_step, s) for s in range(half // 2)], pieces)
 
     mask_all = meta_p[0][:, : pre * n_group]
     sums = meta_p[0][:, 128:]
@@ -368,7 +373,7 @@
                 forward_sums(i - 3, held.pop(("a", i - 3)))
 
     for k in range(n_chunk):
-        gather_last(k)
+        by_core(gather_last, k)
         forward(*chunks[k])
 
     col_sq = jnp.sum(acc_sq[...], axis=1, keepdims=True)
@@ -467,88 +472,80 @@
     def block(way, dist):
         return away(way, dist)
 
-    def reduce_far(way, s, k):
-        src = part.at[block(way, half - 2 * s), heads_of(k)]
-        dst = r_far.at[way, s, heads_of(k)]
-        to = {"group": away(way, 2)}
-        return remote(src, dst, sf_send.at[way, s, k], sf_recv.at[way, s, k], to)
-
-    def reduce_near(way, s, k):
-        src = part.at[block(way, half - 1 - 2 * s), heads_of(k)]
-        dst = r_near.at[way, s, heads_of(k)]
-        to = {"group": away(way, 1)}
-        return remote(src, dst, sn_send.at[way, s, k], sn_recv.at[way, s, k], to)
-
-    def sends_far(way, s, k):
-        return way == k or s > 0
-
-    def arrived(way, s, k):
+    def reduce_copy(stride, way, dist, k):
+        src = part.at[block(way, dist), heads_of(k)]
+        dst = r_in.at[way, dist - 1, heads_of(k)]
+        at = (way, dist - 1, k)
+        hop = dist - (dist - 1) // stride * stride
+        return remote(src, dst, s_send.at[at], s_recv.at[at], {"group": away(way, hop)})
+
+    def arrived(stride, way, dist, k):
         lo, hi = chunks[k]
-        reduce_near(way, s - 1, k).wait_recv()
-        got = r_near[way, s - 1, lo:hi].astype(F32)
-        if sends_far(way, s - 1, k):
-            reduce_far(way, s - 1, k).wait_recv()
-            got = got + r_far[way, s - 1, lo:hi].astype(F32)
+        got = None
+        for d in range(min(dist + stride, reach(way, k)), dist, -1):
+            reduce_copy(stride, way, d, k).wait_recv()
+            one = r_in[way, d - 1, lo:hi].astype(F32)
+            got = one if got is None else got + one
         return got
 
-    def start_near(s, k):
-        for way in (k, 1 - k):
-            reduce_near(way, s, k).start()
-
-    def reduce_on(s, k):
-        lo, hi = chunks[k]
-        for way in (k, 1 - k):
-            if sends_far(way, s, k):
-                if s > 0:
-                    at = block(way, half - 2 * s)
-                    here = part[at, lo:hi].astype(F32) + arrived(way, s, k)
-                    part[at, lo:hi] = here.astype(BF16)
-                reduce_far(way, s, k).start()
-
-    def reduce_step(s):
+    def joints(stride, way, k):
+        return [d for d in range(reach(way, k) - 1, 0, -1) if d % stride == 0]
+
+    def start_plain(stride, i, k):
+        for way in ways_of(k):
+            at = [reach(way, k) + 1] + joints(stride, way, k) + [0]
+            if i + 1 < len(at):
+                for d in range(at[i] - 1, at[i + 1], -1):
+                    reduce_copy(stride, way, d, k).start()
+
+    def reduce_step(stride, i):
         for k in range(n_chunk):
-            if s > 0:
-                reduce_on(s, k)
-        if s + 1 < steps:
-            for k in range(n_chunk):
-                start_near(s + 1, k)
-
-    def reduce_last(k):
+            lo, hi = chunks[k]
+            for way in ways_of(k):
+                at = joints(stride, way, k)
+                if 0 < i <= len(at):
+                    b = block(way, at[i - 1])
+                    here = part[b, lo:hi].astype(F32) + arrived(stride, way, at[i - 1], k)
+                    part[b, lo:hi] = here.astype(BF16)
+                    reduce_copy(stride, way, at[i - 1], k).start()
+        for k in range(n_chunk):
+            start_plain(stride, i + 1, k)
+
+    def reduce_last(stride, k):
         lo, hi = chunks[k]
         tot = part[g, lo:hi].astype(F32)
-        for way in range(2):
-            tot = tot + arrived(way, steps, k)
+        for way in ways_of(k):
+            tot = tot + arrived(stride, way, 0, k)
         for h in range(lo, hi):
             cols = slice(h * HEAD_DIM, (h + 1) * HEAD_DIM)
             gpk_ref[0, :, cols] = tot[h - lo, :8].astype(BF16)
             gpv_ref[0, :, cols] = tot[h - lo, 8:].astype(BF16)
 
+    def early_sends():
+        for d in range(1, n_group):
+            meta_group(d).wait_send()
+        for d in range(1, n_prompt):
+            meta_prompt(d).wait_send()
+        swap.wait_send()
+
+    def ring_sends(stride, copy):
+        for k in range(n_chunk):
+            for way in ways_of(k):
+                for dist in range(1, reach(way, k) + 1):
+                    copy(stride, way, dist, k).wait_send()
+
     for k in range(n_chunk):
         backward_prefix(*chunks[k])
-        reduce_on(0, k)
-        start_near(0, k)
+        by_core(start_plain, 0, k)
     weave(
-        [functools.partial(reduce_step, s) for s in range(steps)],
+        [functools.partial(by_core, reduce_step, i) for i in range(half // 2)],
         [functools.partial(backward_own, hs) for hs in trios],
     )
+    early_sends()
+    by_core(ring_sends, gather_copy)
     for k in range(n_chunk):
-        reduce_last(k)
-
-    for d in range(1, n_group):
-        meta_group(d).wait_send()
-    for d in range(1, n_prompt):
-        meta_prompt(d).wait_send()
-    swap.wait_send()
-
-    for k in range(n_chunk):
-        for way in range(2):
-            for s in range(steps):
-                if has_far(way, s, k):
-                    gather_far(way, s, k).wait_send()
-                gather_near(way, s, k).wait_send()
-                if sends_far(way, s, k):
-                    reduce_far(way, s, k).wait_send()
-                reduce_near(way, s, k).wait_send()
+        by_core(reduce_last, k)
+    by_core(ring_sends, reduce_copy)
 
 
 def store_kernel(*refs):
@@ -569,7 +566,6 @@
     rows = samp * ROWS
     total_rows = -(-rows // 128) * 128
     half = n_group // 2
-    steps = half // 2
     n_chunk = 2
     hbm = pl.BlockSpec(memory_space=pltpu.HBM)
     vmem = pl.BlockSpec(memory_space=pltpu.VMEM)
@@ -612,21 +608,16 @@
             v((rows, HEAD_DIM), F32),
             v((rows, HEAD_DIM), F32),
             v((n_group,) + slab, BF16),
-            v((2, steps) + slab, BF16),
-            v((2, steps) + slab, BF16),
+            v((2, half) + slab, BF16),
             v((n_group, 1, 256), F32),
             v((n_prompt, 1, 256), F32),
             v((2, 8, total_rows), F32),
             dma((4,)),
             dma((3,)),
-            dma((2, steps, n_chunk)),
-            dma((2, steps, n_chunk)),
-            dma((2, steps, n_chunk)),
-            dma((2, steps, n_chunk)),
-            dma((2, steps, n_chunk)),
-            dma((2, steps, n_chunk)),
-            dma((2, steps, n_chunk)),
-            dma((2, steps, n_chunk)),
+            dma((2, half, n_chunk)),
+            dma((2, half, n_chunk)),
+            dma((2, half, n_chunk)),
+            dma((2, half, n_chunk)),
             dma((n_group,)),
             dma((n_group,)),
             dma((n_prompt,)),

time: 65.2 us -> 65.7 us (level)
  Pallas kernels: 62.6 us -> 63.6 us
    pallas_call x1, Pallas kernels: 61.3 us -> 62.3 us  [body(): pl.pallas_call(functools.partial(layer_kernel, sizes), out_shape=(big, bi...]
where the time goes in v3:
time: 65.7 us; the launch traced here: 65.1 us
  Pallas kernels  63.6 us (97%)
  other arithmetic  0.79 us (1%)
  between operations  0.7 us (1%)
    pallas_call x1, Pallas kernels, body(): pl.pallas_call(functools.partial(layer_kernel, sizes), out_shape=(big, bi...  62.3 us

profile of v3, /device:TPU:24, one launch (start us, length us, event | category | flops | bytes accessed | tf_op | source)
XLA Modules:
  0.0 65.1 jit_solution(16026055014622028629)
XLA Ops:
  0.6 0.0 copy-start
  0.6 0.0 copy-start.3
  0.7 0.0 copy-start.2
  0.7 0.0 copy-start.1
  0.7 0.8 %pad_maximum_fusion.kv_ref = bf16[2,8,1792]{2,1,0:T(8,128)(2,1)S(1)} fusion(bf16[1,8,1792]{2,1,0:T(8,128)(2,1)} %param.15, bf16[1,8,1792]{2,1,0:T(8,128)(2,1)} %param.14), kind=kLoop, calls=%fused_computation | loop fusion | flops 28672 | bytes 114688 | tf_op jit(solution)/shard_map/concatenate | solution.py:576
  1.5 0.0 copy-done
  1.5 0.0 copy-done.3
  1.5 0.0 copy-done.2
  1.5 0.0 copy-done.1
  1.5 62.3 %shard_map.137 = (bf16[1,3,50,1792]{3,2,1,0:T(8,128)(2,1)S(1)}, bf16[1,3,50,1792]{3,2,1,0:T(8,128)(2,1)S(1)}, bf16[1,3,50,1792]{3,2,1,0:T(8,128)(2,1)S(1)}, bf16...) custom-call(s32[1,8]{1,0:T(1,128)S(1)} %copy-done.1, s32[1,3]{1,0:T(1,128)S(1)} %copy-done.2, s32[1,3]{1,0:T(1,128)S(1)} %copy-done.3, ...), custom_call_target="tpu_custom_call" | custom-call | tf_op jit(solution)/shard_map/pallas_call | solution.py:579
  63.8 1.3 %shard_map.138 = (bf16[1,3,50,1792]{3,2,1,0:T(8,128)(2,1)}, bf16[1,3,50,1792]{3,2,1,0:T(8,128)(2,1)}, bf16[1,3,50,1792]{3,2,1,0:T(8,128)(2,1)}, bf16[1,8,1792]{2,1,0:T(8,128)(2,1)}, bf16[1,8,1792]{2,1,0:T(8,128)(2,1)}) custom-call(bf16[1,3,50,1792]{3,2,1,0:T(8,128)(2,1)S(1)} %get-tuple-element.10.refs_0_, ...), custom_call_target="tpu_custom_call" | custom-call | tf_op jit(solution)/shard_map/pallas_call | solution.py:632
Async XLA Ops:
  0.6 0.8 %copy-start = (bf16[1792]{0:T(1024)(128)(2,1)S(1)}, bf16[1792]{0:T(1024)(128)(2,1)}, u32[]{:S(2)}) copy-start(bf16[1792]{0:T(1024)(128)(2,1)} %gain_ref.1) | copy-start | bytes 10756
  0.6 0.8 %copy-start.3 = (s32[1,3]{1,0:T(1,128)S(1)}, s32[1,3]{1,0:T(1,128)}, u32[]{:S(2)}) copy-start(s32[1,3]{1,0:T(1,128)} %rew_hbm.1) | copy-start | bytes 40
  0.7 0.8 %copy-start.2 = (s32[1,3]{1,0:T(1,128)S(1)}, s32[1,3]{1,0:T(1,128)}, u32[]{:S(2)}) copy-start(s32[1,3]{1,0:T(1,128)} %len_hbm.1) | copy-start | bytes 40
  0.7 0.8 %copy-start.1 = (s32[1,8]{1,0:T(1,128)S(1)}, s32[1,8]{1,0:T(1,128)}, u32[]{:S(2)}) copy-start(s32[1,8]{1,0:T(1,128)} %mask_hbm.1) | copy-start | bytes 100

commit v4 on v3

--- a/solution.py
+++ b/solution.py
@@ -108,15 +108,7 @@
     g = lax.axis_index("group")
     p = lax.axis_index("prompt")
     m = lax.axis_index("mp")
-    core = lax.rem(p, 2)
-
-    def by_core(f, *args):
-        for mine, stride in ((0, 3), (1, 2)):
-
-            @pl.when(core == mine)
-            def _(stride=stride):
-                f(stride, *args)
-
+    stride = 2
 
     small = [
         pltpu.make_async_copy(src, dst, small_sem.at[i])
@@ -183,31 +175,34 @@
     def behind(way, dist):
         return away(1 - way, dist)
 
-    def gather_copy(stride, way, dist, k):
+    def gather_copy(way, dist, k):
         held = (dist - 1) // stride * stride
         ref = kvg.at[behind(way, held), heads_of(k)]
         at = (way, dist - 1, k)
         return remote(ref, ref, g_send.at[at], g_recv.at[at], {"group": away(way, dist - held)})
 
-    def gather_step(stride, s):
+    def gather_step(s, k):
         held = stride * s
-        for k in range(n_chunk):
+        for way in ways_of(k):
+            if 0 < held < reach(way, k):
+                gather_copy(way, held, k).wait_recv()
+            if held + stride <= reach(way, k):
+                gather_copy(way, held + stride, k).start()
+        for dist in range(held + stride - 1, held, -1):
             for way in ways_of(k):
-                if 0 < held < reach(way, k):
-                    gather_copy(stride, way, held, k).wait_recv()
-                if held + stride <= reach(way, k):
-                    gather_copy(stride, way, held + stride, k).start()
-        for k in range(n_chunk):
-            for dist in range(held + stride - 1, held, -1):
-                for way in ways_of(k):
-                    if dist <= reach(way, k):
-                        gather_copy(stride, way, dist, k).start()
-
-    def gather_last(stride, k):
+                if dist <= reach(way, k):
+                    gather_copy(way, dist, k).start()
+
+    def gather_steps(s):
+        gather_step(s, 0)
+        if s > 0:
+            gather_step(s - 1, 1)
+
+    def gather_last(k):
         for way in ways_of(k):
             for dist in range(1, reach(way, k) + 1):
                 if dist % stride or dist == reach(way, k):
-                    gather_copy(stride, way, dist, k).wait_recv()
+                    gather_copy(way, dist, k).wait_recv()
 
     def meta_group(d):
         return remote(
@@ -322,7 +317,8 @@
     ]
     trios = [list(range(h, min(h + 3, heads))) for h in range(0, heads, 3)]
     pieces += [functools.partial(own_part, hs) for hs in trios]
-    weave([functools.partial(by_core, gather_step, s) for s in range(half // 2)], pieces)
+    last = half // 2 - 1
+    weave([functools.partial(gather_steps, s) for s in range(last + 1)], pieces)
 
     mask_all = meta_p[0][:, : pre * n_group]
     sums = meta_p[0][:, 128:]
@@ -372,9 +368,11 @@
             if lo <= i - 3 < hi:
                 forward_sums(i - 3, held.pop(("a", i - 3)))
 
-    for k in range(n_chunk):
-        by_core(gather_last, k)
-        forward(*chunks[k])
+    gather_last(0)
+    gather_step(last, 1)
+    forward(*chunks[0])
+    gather_last(1)
+    forward(*chunks[1])
 
     col_sq = jnp.sum(acc_sq[...], axis=1, keepdims=True)
     col_in = jnp.sum(acc_in[...], axis=1, keepdims=True)
@@ -472,50 +470,50 @@
     def block(way, dist):
         return away(way, dist)
 
-    def reduce_copy(stride, way, dist, k):
+    def reduce_copy(way, dist, k):
         src = part.at[block(way, dist), heads_of(k)]
         dst = r_in.at[way, dist - 1, heads_of(k)]
         at = (way, dist - 1, k)
         hop = dist - (dist - 1) // stride * stride
         return remote(src, dst, s_send.at[at], s_recv.at[at], {"group": away(way, hop)})
 
-    def arrived(stride, way, dist, k):
+    def arrived(way, dist, k):
         lo, hi = chunks[k]
         got = None
         for d in range(min(dist + stride, reach(way, k)), dist, -1):
-            reduce_copy(stride, way, d, k).wait_recv()
+            reduce_copy(way, d, k).wait_recv()
             one = r_in[way, d - 1, lo:hi].astype(F32)
             got = one if got is None else got + one
         return got
 
-    def joints(stride, way, k):
+    def joints(way, k):
         return [d for d in range(reach(way, k) - 1, 0, -1) if d % stride == 0]
 
-    def start_plain(stride, i, k):
+    def start_plain(i, k):
         for way in ways_of(k):
-            at = [reach(way, k) + 1] + joints(stride, way, k) + [0]
+            at = [reach(way, k) + 1] + joints(way, k) + [0]
             if i + 1 < len(at):
                 for d in range(at[i] - 1, at[i + 1], -1):
-                    reduce_copy(stride, way, d, k).start()
-
-    def reduce_step(stride, i):
+                    reduce_copy(way, d, k).start()
+
+    def reduce_step(i):
         for k in range(n_chunk):
             lo, hi = chunks[k]
             for way in ways_of(k):
-                at = joints(stride, way, k)
+                at = joints(way, k)
                 if 0 < i <= len(at):
                     b = block(way, at[i - 1])
-                    here = part[b, lo:hi].astype(F32) + arrived(stride, way, at[i - 1], k)
+                    here = part[b, lo:hi].astype(F32) + arrived(way, at[i - 1], k)
                     part[b, lo:hi] = here.astype(BF16)
-                    reduce_copy(stride, way, at[i - 1], k).start()
+                    reduce_copy(way, at[i - 1], k).start()
         for k in range(n_chunk):
-            start_plain(stride, i + 1, k)
-
-    def reduce_last(stride, k):
+            start_plain(i + 1, k)
+
+    def reduce_last(k):
         lo, hi = chunks[k]
         tot = part[g, lo:hi].astype(F32)
         for way in ways_of(k):
-            tot = tot + arrived(stride, way, 0, k)
+            tot = tot + arrived(way, 0, k)
         for h in range(lo, hi):
             cols = slice(h * HEAD_DIM, (h + 1) * HEAD_DIM)
             gpk_ref[0, :, cols] = tot[h - lo, :8].astype(BF16)
@@ -528,24 +526,24 @@
             meta_prompt(d).wait_send()
         swap.wait_send()
 
-    def ring_sends(stride, copy):
+    def ring_sends(copy):
         for k in range(n_chunk):
             for way in ways_of(k):
                 for dist in range(1, reach(way, k) + 1):
-                    copy(stride, way, dist, k).wait_send()
+                    copy(way, dist, k).wait_send()
 
     for k in range(n_chunk):
         backward_prefix(*chunks[k])
-        by_core(start_plain, 0, k)
+        start_plain(0, k)
     weave(
-        [functools.partial(by_core, reduce_step, i) for i in range(half // 2)],
+        [functools.partial(reduce_step, i) for i in range(half // 2)],
         [functools.partial(backward_own, hs) for hs in trios],
     )
     early_sends()
-    by_core(ring_sends, gather_copy)
+    ring_sends(gather_copy)
     for k in range(n_chunk):
-        by_core(reduce_last, k)
-    by_core(ring_sends, reduce_copy)
+        reduce_last(k)
+    ring_sends(reduce_copy)
 
 
 def store_kernel(*refs):

time: 65.7 us -> 67.7 us (1.030)
  Pallas kernels: 63.6 us -> 65.3 us
    pallas_call x1, Pallas kernels: 62.3 us -> 64 us  [body(): pl.pallas_call(functools.partial(layer_kernel, sizes), out_shape=(big, bi...]
where the time goes in v4:
time: 67.7 us; the launch traced here: 66.8 us
  Pallas kernels  65.3 us (96%)
  other arithmetic  0.79 us (1%)
  between operations  0.7 us (1%)
    pallas_call x1, Pallas kernels, body(): pl.pallas_call(functools.partial(layer_kernel, sizes), out_shape=(big, bi...  64 us

profile of v4, /device:TPU:24, one launch (start us, length us, event | category | flops | bytes accessed | tf_op | source)
XLA Modules:
  0.0 66.8 jit_solution(12400966989238698659)
XLA Ops:
  0.6 0.0 copy-start
  0.6 0.0 copy-start.3
  0.7 0.0 copy-start.2
  0.7 0.0 copy-start.1
  0.7 0.8 %pad_maximum_fusion.kv_ref = bf16[2,8,1792]{2,1,0:T(8,128)(2,1)S(1)} fusion(bf16[1,8,1792]{2,1,0:T(8,128)(2,1)} %param.15, bf16[1,8,1792]{2,1,0:T(8,128)(2,1)} %param.14), kind=kLoop, calls=%fused_computation | loop fusion | flops 28672 | bytes 114688 | tf_op jit(solution)/shard_map/concatenate | solution.py:574
  1.5 0.0 copy-done
  1.5 0.0 copy-done.3
  1.5 0.0 copy-done.2
  1.5 0.0 copy-done.1
  1.5 64.0 %shard_map.137 = (bf16[1,3,50,1792]{3,2,1,0:T(8,128)(2,1)S(1)}, bf16[1,3,50,1792]{3,2,1,0:T(8,128)(2,1)S(1)}, bf16[1,3,50,1792]{3,2,1,0:T(8,128)(2,1)S(1)}, bf16...) custom-call(s32[1,8]{1,0:T(1,128)S(1)} %copy-done.1, s32[1,3]{1,0:T(1,128)S(1)} %copy-done.2, s32[1,3]{1,0:T(1,128)S(1)} %copy-done.3, ...), custom_call_target="tpu_custom_call" | custom-call | tf_op jit(solution)/shard_map/pallas_call | solution.py:577
  65.5 1.3 %shard_map.138 = (bf16[1,3,50,1792]{3,2,1,0:T(8,128)(2,1)}, bf16[1,3,50,1792]{3,2,1,0:T(8,128)(2,1)}, bf16[1,3,50,1792]{3,2,1,0:T(8,128)(2,1)}, bf16[1,8,1792]{2,1,0:T(8,128)(2,1)}, bf16[1,8,1792]{2,1,0:T(8,128)(2,1)}) custom-call(bf16[1,3,50,1792]{3,2,1,0:T(8,128)(2,1)S(1)} %get-tuple-element.10.refs_0_, ...), custom_call_target="tpu_custom_call" | custom-call | tf_op jit(solution)/shard_map/pallas_call | solution.py:630
Async XLA Ops:
  0.6 0.8 %copy-start = (bf16[1792]{0:T(1024)(128)(2,1)S(1)}, bf16[1792]{0:T(1024)(128)(2,1)}, u32[]{:S(2)}) copy-start(bf16[1792]{0:T(1024)(128)(2,1)} %gain_ref.1) | copy-start | bytes 10756
  0.6 0.8 %copy-start.3 = (s32[1,3]{1,0:T(1,128)S(1)}, s32[1,3]{1,0:T(1,128)}, u32[]{:S(2)}) copy-start(s32[1,3]{1,0:T(1,128)} %rew_hbm.1) | copy-start | bytes 40
  0.7 0.8 %copy-start.2 = (s32[1,3]{1,0:T(1,128)S(1)}, s32[1,3]{1,0:T(1,128)}, u32[]{:S(2)}) copy-start(s32[1,3]{1,0:T(1,128)} %len_hbm.1) | copy-start | bytes 40
  0.7 0.8 %copy-start.1 = (s32[1,8]{1,0:T(1,128)S(1)}, s32[1,8]{1,0:T(1,128)}, u32[]{:S(2)}) copy-start(s32[1,8]{1,0:T(1,128)} %mask_hbm.1) | copy-start | bytes 100

commit v5 on v3

--- a/solution.py
+++ b/solution.py
@@ -110,8 +110,16 @@
     m = lax.axis_index("mp")
     core = lax.rem(p, 2)
 
+    def base(stride, dist):
+        return max(h for h in stride if h < dist)
+
+    def after(stride, dist):
+        return min([h for h in stride if h > dist] + [half])
+
     def by_core(f, *args):
-        for mine, stride in ((0, 3), (1, 2)):
+        evens = tuple(range(0, half, 2))
+        mixed = tuple(h for h in range(half) if h % 2 == 0 or h > half // 2)
+        for mine, stride in ((0, evens), (1, mixed)):
 
             @pl.when(core == mine)
             def _(stride=stride):
@@ -184,21 +192,24 @@
         return away(1 - way, dist)
 
     def gather_copy(stride, way, dist, k):
-        held = (dist - 1) // stride * stride
+        held = base(stride, dist)
         ref = kvg.at[behind(way, held), heads_of(k)]
         at = (way, dist - 1, k)
         return remote(ref, ref, g_send.at[at], g_recv.at[at], {"group": away(way, dist - held)})
 
     def gather_step(stride, s):
-        held = stride * s
+        if s >= len(stride):
+            return
+        held = stride[s]
+        top = after(stride, held)
         for k in range(n_chunk):
             for way in ways_of(k):
                 if 0 < held < reach(way, k):
                     gather_copy(stride, way, held, k).wait_recv()
-                if held + stride <= reach(way, k):
-                    gather_copy(stride, way, held + stride, k).start()
+                if top <= reach(way, k):
+                    gather_copy(stride, way, top, k).start()
         for k in range(n_chunk):
-            for dist in range(held + stride - 1, held, -1):
+            for dist in range(top - 1, held, -1):
                 for way in ways_of(k):
                     if dist <= reach(way, k):
                         gather_copy(stride, way, dist, k).start()
@@ -206,7 +217,7 @@
     def gather_last(stride, k):
         for way in ways_of(k):
             for dist in range(1, reach(way, k) + 1):
-                if dist % stride or dist == reach(way, k):
+                if dist not in stride or dist == reach(way, k):
                     gather_copy(stride, way, dist, k).wait_recv()
 
     def meta_group(d):
@@ -322,7 +333,7 @@
     ]
     trios = [list(range(h, min(h + 3, heads))) for h in range(0, heads, 3)]
     pieces += [functools.partial(own_part, hs) for hs in trios]
-    weave([functools.partial(by_core, gather_step, s) for s in range(half // 2)], pieces)
+    weave([functools.partial(by_core, gather_step, s) for s in range(half - 2)], pieces)
 
     mask_all = meta_p[0][:, : pre * n_group]
     sums = meta_p[0][:, 128:]
@@ -476,20 +487,20 @@
         src = part.at[block(way, dist), heads_of(k)]
         dst = r_in.at[way, dist - 1, heads_of(k)]
         at = (way, dist - 1, k)
-        hop = dist - (dist - 1) // stride * stride
+        hop = dist - base(stride, dist)
         return remote(src, dst, s_send.at[at], s_recv.at[at], {"group": away(way, hop)})
 
     def arrived(stride, way, dist, k):
         lo, hi = chunks[k]
         got = None
-        for d in range(min(dist + stride, reach(way, k)), dist, -1):
+        for d in range(min(after(stride, dist), reach(way, k)), dist, -1):
             reduce_copy(stride, way, d, k).wait_recv()
             one = r_in[way, d - 1, lo:hi].astype(F32)
             got = one if got is None else got + one
         return got
 
     def joints(stride, way, k):
-        return [d for d in range(reach(way, k) - 1, 0, -1) if d % stride == 0]
+        return [d for d in range(reach(way, k) - 1, 0, -1) if d in stride]
 
     def start_plain(stride, i, k):
         for way in ways_of(k):
@@ -538,7 +549,7 @@
         backward_prefix(*chunks[k])
         by_core(start_plain, 0, k)
     weave(
-        [functools.partial(by_core, reduce_step, i) for i in range(half // 2)],
+        [functools.partial(by_core, reduce_step, i) for i in range(half - 2)],
         [functools.partial(backward_own, hs) for hs in trios],
     )
     early_sends()

time: 65.7 us -> 66.3 us (level)
  the two profiles are of different devices: /device:TPU:24 before, /device:TPU:1 now
where the time goes in v5:
time: 66.3 us; the launch traced here: 66.1 us
  Pallas kernels  64.6 us (97%)
  other arithmetic  0.79 us (1%)
  between operations  0.7 us (1%)
    pallas_call x1, Pallas kernels, body(): pl.pallas_call(functools.partial(layer_kernel, sizes), out_shape=(big, bi...  63.3 us

profile of v5, /device:TPU:1, one launch (start us, length us, event | category | flops | bytes accessed | tf_op | source)
XLA Modules:
  0.0 66.1 jit_solution(16190452214702574102)
XLA Ops:
  0.6 0.0 copy-start
  0.6 0.0 copy-start.3
  0.7 0.0 copy-start.2
  0.7 0.0 copy-start.1
  0.7 0.8 %pad_maximum_fusion.kv_ref = bf16[2,8,1792]{2,1,0:T(8,128)(2,1)S(1)} fusion(bf16[1,8,1792]{2,1,0:T(8,128)(2,1)} %param.15, bf16[1,8,1792]{2,1,0:T(8,128)(2,1)} %param.14), kind=kLoop, calls=%fused_computation | loop fusion | flops 28672 | bytes 114688 | tf_op jit(solution)/shard_map/concatenate | solution.py:587
  1.5 0.0 copy-done
  1.5 0.0 copy-done.3
  1.5 0.0 copy-done.2
  1.5 0.0 copy-done.1
  1.5 63.3 %shard_map.137 = (bf16[1,3,50,1792]{3,2,1,0:T(8,128)(2,1)S(1)}, bf16[1,3,50,1792]{3,2,1,0:T(8,128)(2,1)S(1)}, bf16[1,3,50,1792]{3,2,1,0:T(8,128)(2,1)S(1)}, bf16...) custom-call(s32[1,8]{1,0:T(1,128)S(1)} %copy-done.1, s32[1,3]{1,0:T(1,128)S(1)} %copy-done.2, s32[1,3]{1,0:T(1,128)S(1)} %copy-done.3, ...), custom_call_target="tpu_custom_call" | custom-call | tf_op jit(solution)/shard_map/pallas_call | solution.py:590
  64.8 1.3 %shard_map.138 = (bf16[1,3,50,1792]{3,2,1,0:T(8,128)(2,1)}, bf16[1,3,50,1792]{3,2,1,0:T(8,128)(2,1)}, bf16[1,3,50,1792]{3,2,1,0:T(8,128)(2,1)}, bf16[1,8,1792]{2,1,0:T(8,128)(2,1)}, bf16[1,8,1792]{2,1,0:T(8,128)(2,1)}) custom-call(bf16[1,3,50,1792]{3,2,1,0:T(8,128)(2,1)S(1)} %get-tuple-element.10.refs_0_, ...), custom_call_target="tpu_custom_call" | custom-call | tf_op jit(solution)/shard_map/pallas_call | solution.py:643
Async XLA Ops:
  0.6 0.8 %copy-start = (bf16[1792]{0:T(1024)(128)(2,1)S(1)}, bf16[1792]{0:T(1024)(128)(2,1)}, u32[]{:S(2)}) copy-start(bf16[1792]{0:T(1024)(128)(2,1)} %gain_ref.1) | copy-start | bytes 10756
  0.6 0.8 %copy-start.3 = (s32[1,3]{1,0:T(1,128)S(1)}, s32[1,3]{1,0:T(1,128)}, u32[]{:S(2)}) copy-start(s32[1,3]{1,0:T(1,128)} %rew_hbm.1) | copy-start | bytes 40
  0.7 0.8 %copy-start.2 = (s32[1,3]{1,0:T(1,128)S(1)}, s32[1,3]{1,0:T(1,128)}, u32[]{:S(2)}) copy-start(s32[1,3]{1,0:T(1,128)} %len_hbm.1) | copy-start | bytes 40
  0.7 0.8 %copy-start.1 = (s32[1,8]{1,0:T(1,128)S(1)}, s32[1,8]{1,0:T(1,128)}, u32[]{:S(2)}) copy-start(s32[1,8]{1,0:T(1,128)} %mask_hbm.1) | copy-start | bytes 100
